TPU v7x, 32 devices: a whole 2x2x4 slice. The times are simulated.
32 devices in a mesh: row: 8 (over y, x, core), col: 4 (over z).
Axes of the slice: x: 2, y: 2, z: 4, core: 2. Of those that a mesh axis runs over, the one named last changes fastest.
Arguments:
- features: float32 [8192, 256], P(('row', 'col')), may hold values from -6 to 6
- new_features: float32 [2048, 256], P(('row', 'col')), may hold values from -6 to 6
- lengths: int32 [8192], P(('row', 'col')), may hold values from 1 to 64
- targets: float32 [8192, 64], P(('row', 'col')), may hold values from -6 to 6
- prior_train: float32 [8192, 256], P(('row', 'col')), may hold values from -6 to 6
- noise_draw: float32 [8192, 256], P(('row', 'col')), may hold values from -6 to 6
- prior_new: float32 [2048, 256], P(('row', 'col')), may hold values from -6 to 6
- time_kernel: float32 [64, 64], replicated, may hold values from -16 to 16.5, as said below
- noise_var: float32 [64], replicated, may hold values from 0.05 to 0.5
Outputs:
- residual: float32 [8192, 256], P(('row', 'col'))
- predicted: float32 [2048, 256], P(('row', 'col'))
Inputs may be any that keep to these rules, and one draw needn't show every extreme that they name: `time_kernel`: symmetric positive definite.
All inputs are finite; a program needn't handle non-finite values.
Results may differ from a plain program's by a relative error of at most 0.00022.
Values sent between devices are 32-bit elements; how exact they have to be, the bound alone decides.
A program may use at most 128 MiB of HBM per device.

v0:
```python
import jax
import jax.numpy as jnp
from jax import lax
from jax.sharding import PartitionSpec as P

ITERS = 2


def unit_rows(values):
    return values / jnp.sqrt(jnp.sum(values * values, axis=1, keepdims=True) + 1e-06)


def kernel(left, right):
    inner = lax.dot_general(left, right, (((1,), (1,)), ((), ())), precision=lax.Precision.HIGHEST)
    return inner + inner * inner * inner


def shards(
    features,
    new_features,
    lengths,
    targets,
    prior_train,
    noise_draw,
    prior_new,
    time_kernel,
    noise_var,
):
    checkpoints = time_kernel.shape[0]
    samples = prior_train.shape[1] // checkpoints
    normed = unit_rows(features)
    normed_new = unit_rows(new_features)
    row_block, row_new = (
        lax.all_gather(normed, "col", axis=0, tiled=True),
        lax.all_gather(normed_new, "col", axis=0, tiled=True),
    )
    column_set = lax.all_gather(normed, "row", axis=0, tiled=True)
    mixing = jnp.kron(jnp.eye(samples, dtype=jnp.float32), time_kernel)
    position = jnp.arange(samples * checkpoints, dtype=jnp.int32) % checkpoints
    mask = (position[None, :] < lengths[:, None]).astype(jnp.float32)
    noise_cols = jnp.tile(noise_var, samples)
    rhs = mask * (jnp.tile(targets, (1, samples)) - prior_train - jnp.sqrt(noise_cols) * noise_draw)
    kernel_tile = kernel(row_block, column_set)

    def operate(direction):
        mixed = jnp.dot(direction, mixing, precision=lax.Precision.HIGHEST)
        spread = lax.all_gather(mixed, "row", axis=0, tiled=True)
        product = lax.psum_scatter(
            jnp.dot(kernel_tile, spread, precision=lax.Precision.HIGHEST),
            "col",
            scatter_dimension=0,
            tiled=True,
        )
        return mask * product + noise_cols * direction

    def per_sample(first, second):
        return jnp.sum((first * second).reshape(first.shape[0], samples, checkpoints), axis=(0, 2))

    def two_products(values, image):
        return lax.psum((per_sample(values, values), per_sample(values, image)), ("row", "col"))

    solution = jnp.zeros_like(rhs)
    residual = rhs
    image = operate(residual)
    norm_now, product = two_products(residual, image)
    alpha = norm_now / product
    direction = residual
    along = image
    for step in range(ITERS):
        spread_alpha = jnp.repeat(alpha, checkpoints)
        solution = solution + spread_alpha * direction
        residual = residual - spread_alpha * along
        if step + 1 < ITERS:
            image = operate(residual)
            norm_next, product = two_products(residual, image)
            ratio = norm_next / norm_now
            alpha = norm_next / (product - ratio * norm_next / alpha)
            spread_ratio = jnp.repeat(ratio, checkpoints)
            direction = residual + spread_ratio * direction
            along = image + spread_ratio * along
            norm_now = norm_next
    mixed_solution = jnp.dot(solution, mixing, precision=lax.Precision.HIGHEST)
    gathered = lax.all_gather(mixed_solution, "row", axis=0, tiled=True)
    cross = kernel(row_new, column_set)
    predicted = prior_new + lax.psum_scatter(
        jnp.dot(cross, gathered, precision=lax.Precision.HIGHEST),
        "col",
        scatter_dimension=0,
        tiled=True,
    )
    return (residual, predicted)


def solution(mesh):
    return jax.shard_map(
        shards,
        mesh=mesh,
        in_specs=(
            P(("row", "col"), None),
            P(("row", "col"), None),
            P(("row", "col")),
            P(("row", "col"), None),
            P(("row", "col"), None),
            P(("row", "col"), None),
            P(("row", "col"), None),
            P(),
            P(),
        ),
        out_specs=(P(("row", "col"), None), P(("row", "col"), None)),
        check_vma=False,
    )
```

profile of v0, /device:TPU:0, one launch (start us, length us, event | category | flops | bytes accessed | tf_op | source)
XLA Modules:
  0.0 350.4 jit_solution(12656938561519485176)
XLA Ops:
  7.3 1.1 multiply_reduce_fusion.3
  8.4 1.8 broadcast_divide_fusion
  10.2 0.7 all-gather.8.cloned.1.call-update
  11.0 0.7 tile.20
  11.6 0.1 tile.21
  11.7 0.9 tile.8
  12.6 0.1 copy.13
  12.7 0.1 broadcast_multiply_fusion
  12.9 0.3 mul.146
  13.3 0.1 compare_select_fusion.2
  13.4 1.1 fusion.17
  14.5 26.4 %all-gather.6.cloned.1.call-done = f32[1024,256]{1,0:T(8,128)} async-done(((f32[256,256]{1,0:T(8,128)}), f32[1024,256]{1,0:T(8,128)}) %all-gather.6.cloned.1.call-update) | async-done | bytes 1048592 | tf_op jit(solution)/shard_map/all_gather | solution.py:34
  40.9 29.3 %all-gather.8.cloned.1.call-done = f32[2048,256]{1,0:T(8,128)} async-done(((f32[256,256]{1,0:T(8,128)}), f32[2048,256]{1,0:T(8,128)}) %all-gather.8.cloned.1.call-update) | async-done | bytes 2097168 | tf_op jit(solution)/shard_map/all_gather | solution.py:37
  70.2 10.5 %fusion.16 = f32[1024,2048]{1,0:T(8,128)} fusion(f32[1024,256]{1,0:T(8,128)} %all-gather.6.cloned.1.call-done, f32[2048,256]{1,0:T(8,128)} %all-gather.8.cloned.1.call-done), kind=kOutput, calls=%fused_computation.37 | convolution fusion | flops 6442450944 | bytes 11534336 | tf_op jit(solution)/shard_map/dot_general | solution.py:14
  80.8 19.9 %all-gather.10.cloned.1.call-done = f32[2048,256]{1,0:T(8,128)} async-done(((f32[256,256]{1,0:T(8,128)}), f32[2048,256]{1,0:T(8,128)}) %all-gather.10.cloned.1.call-update) | async-done | bytes 2097168 | tf_op jit(solution)/shard_map/all_gather | solution.py:47
  100.6 11.2 %fusion.1 = f32[1024,256]{1,0:T(8,128)} fusion(f32[2048,256]{1,0:T(8,128)} %all-gather.10.cloned.1.call-done, f32[1024,2048]{1,0:T(8,128)} %fusion.16), kind=kOutput, calls=%fused_computation.2 | convolution fusion | flops 6448742400 | bytes 11534336 | tf_op jit(solution)/shard_map/dot_general | solution.py:49
  111.9 27.2 %reduce-scatter.4.cloned.1.call-done = f32[256,256]{1,0:T(8,128)} async-done(((f32[1024,256]{1,0:T(8,128)}), f32[256,256]{1,0:T(8,128)}) %reduce-scatter.4.cloned.1.call-update) | async-done | bytes 262160 | tf_op jit(solution)/shard_map/reduce_scatter | solution.py:48
  139.2 1.1 multiply_reduce_fusion.2
  140.2 0.1 reduce_sum.66
  140.3 0.1 reduce_sum.73
  140.4 0.1 reduce_sum.67
  140.5 0.1 reduce_sum.88
  140.6 38.9 %all-reduce.1 = (f32[4]{0:T(128)S(1)}, f32[4]{0:T(128)S(1)}) all-reduce(f32[4]{0:T(128)S(1)} %reduce_sum.67, f32[4]{0:T(128)S(1)} %reduce_sum.88), channel_id=1, replica_groups=mesh['row'=8,'col'=4] {'row','col'}, use_global_device_ids=true, to_apply=%region_2.3 | all-reduce | flops 8 | bytes 64 | tf_op jit(solution)/shard_map/psum | solution.py:60
  179.5 0.1 broadcast_in_dim.10
  179.6 0.1 mul.151
  179.7 2.1 fusion.15
  181.8 0.2 reduce-scatter.6.cloned.1.call-start
  182.0 27.6 %all-gather.12.cloned.1.call-done = f32[2048,256]{1,0:T(8,128)} async-done(((f32[256,256]{1,0:T(8,128)}), f32[2048,256]{1,0:T(8,128)}) %all-gather.12.cloned.1.call-update) | async-done | bytes 2097168 | tf_op jit(solution)/shard_map/all_gather | solution.py:47
  209.6 11.2 %fusion = f32[1024,256]{1,0:T(8,128)} fusion(f32[2048,256]{1,0:T(8,128)} %all-gather.12.cloned.1.call-done, f32[1024,2048]{1,0:T(8,128)} %fusion.16), kind=kOutput, calls=%fused_computation.1 | convolution fusion | flops 6448742400 | bytes 11534336 | tf_op jit(solution)/shard_map/dot_general | solution.py:49
  220.9 27.2 %reduce-scatter.6.cloned.1.call-done = f32[256,256]{1,0:T(8,128)} async-done(((f32[1024,256]{1,0:T(8,128)}), f32[256,256]{1,0:T(8,128)}) %reduce-scatter.6.cloned.1.call-update) | async-done | bytes 262160 | tf_op jit(solution)/shard_map/reduce_scatter | solution.py:48
  248.1 1.1 multiply_reduce_fusion
  249.2 0.1 reduce_sum.90
  249.3 0.1 reduce_sum.91
  249.4 0.1 reduce_sum.93
  249.5 0.1 reduce_sum.94
  249.7 38.9 %all-reduce = (f32[4]{0:T(128)S(1)}, f32[4]{0:T(128)S(1)}) all-reduce(f32[4]{0:T(128)S(1)} %reduce_sum.91, f32[4]{0:T(128)S(1)} %reduce_sum.94), channel_id=1, replica_groups=mesh['row'=8,'col'=4] {'row','col'}, use_global_device_ids=true, to_apply=%region_10.11 | all-reduce | flops 8 | bytes 64 | tf_op jit(solution)/shard_map/psum | solution.py:60
  288.6 0.1 mul.159
  288.8 0.1 mul.161
  288.9 1.2 fusion.5
  290.1 0.1 multiply_reduce_fusion.5
  290.2 0.1 broadcast_divide_fusion.1
  290.3 14.4 %all_gather.22 = f32[256,256]{1,0:T(8,128)S(1)} all-gather(f32[64,256]{1,0:T(8,128)S(1)} %broadcast_divide_fusion.1), channel_id=1, replica_groups=mesh['row'=8,'col'=4] {'col'}, dimensions={0}, use_global_device_ids=true | all-gather | bytes 327680 | tf_op jit(solution)/shard_map/all_gather | solution.py:35
  304.7 3.5 %fusion.18 = f32[256,2048]{1,0:T(8,128)S(1)} fusion(f32[256,256]{1,0:T(8,128)S(1)} %all_gather.22, f32[2048,256]{1,0:T(8,128)} %all-gather.8.cloned.1.call-done), kind=kOutput, calls=%fused_computation.39 | convolution fusion | flops 1610612736 | bytes 4456448 | tf_op jit(solution)/shard_map/dot_general | solution.py:14
  308.3 9.6 %all-gather.14.cloned.1.call-done = f32[2048,256]{1,0:T(8,128)} async-done(((f32[256,256]{1,0:T(8,128)}), f32[2048,256]{1,0:T(8,128)}) %all-gather.14.cloned.1.call-update) | async-done | bytes 2097168 | tf_op jit(solution)/shard_map/all_gather | solution.py:83
  317.9 4.4 %fusion.2 = f32[256,256]{1,0:T(8,128)} fusion(f32[2048,256]{1,0:T(8,128)} %all-gather.14.cloned.1.call-done, f32[256,2048]{1,0:T(8,128)S(1)} %fusion.18), kind=kOutput, calls=%fused_computation.4 | convolution fusion | flops 1612185600 | bytes 4456448 | tf_op jit(solution)/shard_map/dot_general | solution.py:86
  322.3 0.9 multiply_subtract_fusion
  323.2 18.9 %reduce-scatter.8.cloned.1.call-done = f32[64,256]{1,0:T(8,128)} async-done(((f32[256,256]{1,0:T(8,128)}), f32[64,256]{1,0:T(8,128)}) %reduce-scatter.8.cloned.1.call-update) | async-done | bytes 65552 | tf_op jit(solution)/shard_map/reduce_scatter | solution.py:85
  342.1 1.5 add.82
  (39 shorter events, 0.6 us)
Async XLA Ops:
  7.2 5.6 %copy-start.7 = (f32[64,64]{1,0:T(8,128)S(1)}, f32[64,64]{1,0:T(8,128)}, u32[]{:S(2)}) copy-start(f32[64,64]{1,0:T(8,128)} %param.16) | copy-start | bytes 49156
  7.2 6.1 %copy-start.6 = (s32[256]{0:T(256)S(1)}, s32[256]{0:T(256)}, u32[]{:S(2)}) copy-start(s32[256]{0:T(256)} %param.11) | copy-start | bytes 3076
  7.2 6.1 %copy-start.3 = (f32[256,256]{1,0:T(8,128)S(1)}, f32[256,256]{1,0:T(8,128)}, u32[]{:S(2)}) copy-start(f32[256,256]{1,0:T(8,128)} %param.13) | copy-start | bytes 786436
  7.2 6.1 %copy-start.2 = (f32[256,256]{1,0:T(8,128)S(1)}, f32[256,256]{1,0:T(8,128)}, u32[]{:S(2)}) copy-start(f32[256,256]{1,0:T(8,128)} %param.14) | copy-start | bytes 786436
  7.2 33.7 %all-gather.6.cloned.1.call-start = ((), (), s32[]{:S(2)}) async-start(), calls=%async_computation.3 | async-start | bytes 1310720 | tf_op jit(solution)/shard_map/all_gather | solution.py:34
  10.2 60.1 %all-gather.8.cloned.1.call-start = ((), (), s32[]{:S(2)}) async-start(), calls=%async_computation.4 | async-start | bytes 2359296 | tf_op jit(solution)/shard_map/all_gather | solution.py:37
  10.9 89.7 %all-gather.10.cloned.1.call-start = ((), (), s32[]{:S(2)}) async-start(), calls=%async_computation.5 | async-start | bytes 2359296 | tf_op jit(solution)/shard_map/all_gather | solution.py:47
  14.5 124.7 %reduce-scatter.4.cloned.1.call-start = ((), (), s32[]{:S(2)}) async-start(), calls=%async_computation.6 | async-start | bytes 1310720 | tf_op jit(solution)/shard_map/reduce_scatter | solution.py:48
  111.9 97.7 %all-gather.12.cloned.1.call-start = ((), (), s32[]{:S(2)}) async-start(), calls=%async_computation.7 | async-start | bytes 2359296 | tf_op jit(solution)/shard_map/all_gather | solution.py:47
  181.8 66.3 %copy-start = (f32[256,256]{1,0:T(8,128)S(1)}, f32[256,256]{1,0:T(8,128)}, u32[]{:S(2)}) copy-start(f32[256,256]{1,0:T(8,128)} %reduce-scatter.4.cloned.1.call-done) | copy-start | bytes 786436
  181.8 66.3 %reduce-scatter.6.cloned.1.call-start = ((), (), s32[]{:S(2)}) async-start(), calls=%async_computation.8 | async-start | bytes 1310720 | tf_op jit(solution)/shard_map/reduce_scatter | solution.py:48
  220.8 69.3 %copy-start.4 = (f32[64,256]{1,0:T(8,128)S(1)}, f32[64,256]{1,0:T(8,128)}, u32[]{:S(2)}) copy-start(f32[64,256]{1,0:T(8,128)} %param.10) | copy-start | bytes 196612
  220.8 97.1 %all-gather.14.cloned.1.call-start = ((), (), s32[]{:S(2)}) async-start(), calls=%async_computation.9 | async-start | bytes 2359296 | tf_op jit(solution)/shard_map/all_gather | solution.py:83
  290.1 52.0 %reduce-scatter.8.cloned.1.call-start = ((), (), s32[]{:S(2)}) async-start(), calls=%async_computation.10 | async-start | bytes 327680 | tf_op jit(solution)/shard_map/reduce_scatter | solution.py:85
  308.2 14.0 %copy-start.1 = (f32[256,256]{1,0:T(8,128)S(1)}, f32[256,256]{1,0:T(8,128)}, u32[]{:S(2)}) copy-start(f32[256,256]{1,0:T(8,128)} %reduce-scatter.6.cloned.1.call-done) | copy-start | bytes 786436
  308.3 33.8 %copy-start.5 = (f32[64,256]{1,0:T(8,128)S(1)}, f32[64,256]{1,0:T(8,128)}, u32[]{:S(2)}) copy-start(f32[64,256]{1,0:T(8,128)} %param.15) | copy-start | bytes 196612
Sparse Core Ops, SparseCore 0:
  10.3 30.6 all-gather.5
  42.8 27.3 all-gather.7
  72.7 27.8 all-gather.9
  112.0 27.1 reduce-scatter.3
  181.9 27.6 all-gather.11
  220.9 27.1 reduce-scatter.5
  290.2 27.6 all-gather.13
  322.4 19.6 reduce-scatter.7
where the time goes:
time: 351 us; the launch traced here: 350 us
  waiting for transfers between devices  187 us (53%)
  blocking collectives  92.1 us (26%)
  matrix products  45.1 us (13%)
  between operations  14.3 us (4%)
  other arithmetic  8.39 us (2%)
    psum x2, blocking collectives, two_products(): lax.psum((per_sample(values, values), per_sample(values, image)), ('row',...  77.8 us
    reduce_scatter x2, waiting for transfers between devices, operate(): lax.psum_scatter(jnp.dot(kernel_tile, spread, precision=lax.Precision.HIG...  54.5 us
    all_gather x2, waiting for transfers between devices, operate(): spread = lax.all_gather(mixed, 'row', axis=0, tiled=True)  47.5 us
    all_gather x1, waiting for transfers between devices, shards(): column_set = lax.all_gather(normed, 'row', axis=0, tiled=True)  29.3 us
    all_gather x1, waiting for transfers between devices, shards(): lax.all_gather(normed, 'col', axis=0, tiled=True)  26.4 us
    dot_general x2, matrix products, operate(): jnp.dot(kernel_tile, spread, precision=lax.Precision.HIGHEST)  22.4 us
    reduce_scatter x1, waiting for transfers between devices, shards(): lax.psum_scatter(jnp.dot(cross, gathered, precision=lax.Precision.HIGHEST...  18.9 us
    all_gather x1, blocking collectives, shards(): lax.all_gather(normed_new, 'col', axis=0, tiled=True)  14.4 us
  transfers between devices with their start and end apart: 8, of which 8 were waited for; matrix products, arithmetic and copies ran while one was open for 5% of the time, Pallas kernels for 0%

commit v1 on v0

v1 whole, which is shorter than its diff:
```python
import functools

import jax
import jax.numpy as jnp
from jax import lax
from jax.experimental import pallas as pl
from jax.experimental.pallas import tpu as pltpu
from jax.sharding import PartitionSpec as P

MESH = pl.DeviceIdType.MESH
F32 = jnp.float32
BF16 = jnp.bfloat16
HIGHEST = lax.Precision.HIGHEST


def split(values):
    high = values.astype(BF16)
    return high, (values - high.astype(F32)).astype(BF16)


def dot3(left, right, dims):
    def one(a, b):
        return lax.dot_general(a, b, (dims, ((), ())), preferred_element_type=F32)

    return one(left[0], right[0]) + (one(left[0], right[1]) + one(left[1], right[0]))


NT = ((1,), (1,))
NN = ((1,), (0,))


def dot_full(a, b, dims=NN):
    return lax.dot_general(a, b, (dims, ((), ())), precision=HIGHEST, preferred_element_type=F32)


def unit_rows(values):
    return values / jnp.sqrt(jnp.sum(values * values, axis=1, keepdims=True) + 1e-06)


def cubic(inner):
    return inner + inner * inner * inner


def body(
    rows,
    cols,
    keep,
    feat,
    feat_new,
    lengths,
    targets,
    prior,
    draw,
    prior_new,
    time_kernel,
    noise_var,
    out_res,
    out_pred,
    ncol,
    nrow,
    nnew,
    v0,
    v1,
    nch,
    ncl,
    kh,
    kl,
    vh,
    vl,
    xacc,
    got,
    xgot,
    rhs_ref,
    mask_ref,
    image_ref,
    mix_ref,
    dots_row,
    dots_col,
    n_send,
    n_recv,
    v_send,
    v_recv,
    z_send,
    z_recv,
    w_send,
    w_recv,
    rs_send,
    rs_recv,
    xs_send,
    xs_recv,
    dr_send,
    dr_recv,
    dc_send,
    dc_recv,
):
    block = feat.shape[0]
    fresh = feat_new.shape[0]
    width = prior.shape[1]
    points = time_kernel.shape[0]
    half = rows // 2
    r = lax.axis_index("row")
    c = lax.axis_index("col")
    pair, core = r // 2, lax.rem(r, 2)
    mate = 2 * pair + 1 - core

    def loop(low, high, step):
        def run(k, carry):
            step(k)
            return carry

        lax.fori_loop(low, high, run, 0)

    def remote(src, dst, send, recv, row, col):
        return pltpu.make_async_remote_copy(
            src_ref=src,
            dst_ref=dst,
            send_sem=send,
            recv_sem=recv,
            device_id=(row, col),
            device_id_type=MESH,
        )

    barrier = pltpu.get_barrier_semaphore()

    def greet_row(k):
        pl.semaphore_signal(barrier, inc=1, device_id=(lax.rem(r + k, rows), c), device_id_type=MESH)

    def greet_col(k):
        pl.semaphore_signal(barrier, inc=1, device_id=(r, lax.rem(c + k, cols)), device_id_type=MESH)

    loop(1, rows, greet_row)
    loop(1, cols, greet_col)

    normed = unit_rows(feat[...])
    ncol[r] = normed
    nrow[c] = normed
    nnew[c] = unit_rows(feat_new[...])

    pl.semaphore_wait(barrier, rows + cols - 2)

    def spread_start(buf, send, recv):
        def to_pair(k):
            there = 2 * lax.rem(pair + k, half) + core
            remote(buf.at[r], buf.at[r], send.at[k], recv.at[r], there, c).start()

        loop(1, half, to_pair)
        remote(buf.at[r], buf.at[r], send.at[0], recv.at[r], mate, c).start()

    def like(k):
        return 2 * lax.rem(pair + half - k, half) + core

    def unlike(k):
        return 2 * lax.rem(pair + half - k, half) + 1 - core

    def spread_forward(buf, send, recv, use):
        def one(k):
            j = like(k)
            fwd = remote(buf.at[j], buf.at[j], send.at[half - 1 + k], recv.at[j], mate, c)
            fwd.wait_recv()
            fwd.start()
            use(j)

        loop(1, half, one)

    def spread_rest(buf, send, recv, use):
        def one(k):
            j = unlike(k)
            remote(buf.at[j], buf.at[j], send.at[0], recv.at[j], mate, c).wait_recv()
            use(j)

        loop(0, half, one)

    def spread_end(buf, send, recv):
        def one(k):
            remote(buf.at[r], buf.at[r], send.at[k], recv.at[r], mate, c).wait_send()

        loop(0, rows - 1, one)

    def line_start(src_of, dst, send, recv):
        def one(k):
            there = lax.rem(c + k, cols)
            remote(src_of(there), dst.at[c], send.at[k], recv.at[c], r, there).start()

        loop(1, cols, one)

    def line_wait(dst, send, recv, k):
        src = lax.rem(c + cols - k, cols)
        remote(dst.at[src], dst.at[src], send.at[k], recv.at[src], r, lax.rem(c + k, cols)).wait_recv()
        return src

    def line_end(dst, send, recv):
        def one(k):
            there = lax.rem(c + k, cols)
            remote(dst.at[c], dst.at[c], send.at[k], recv.at[c], r, there).wait_send()

        loop(1, cols, one)

    line_start(lambda there: nrow.at[c], nrow, z_send, z_recv)
    spread_start(ncol, n_send, n_recv)
    line_start(lambda there: nnew.at[c], nnew, w_send, w_recv)

    lane = lax.broadcasted_iota(jnp.int32, (points, width), 1)
    line = lax.broadcasted_iota(jnp.int32, (points, width), 0)
    repeat = (lax.rem(lane, points) == line).astype(F32)
    wide_row = lax.broadcasted_iota(jnp.int32, (width, width), 0) // points
    wide_col = lax.broadcasted_iota(jnp.int32, (width, width), 1) // points
    same = (wide_row == wide_col).astype(F32)
    mix_ref[...] = same * dot_full(repeat, dot_full(time_kernel[...], repeat), ((0,), (0,)))
    noise_cols = dot_full(jnp.broadcast_to(noise_var[...], (8, points)), repeat)[0:1]
    place = lax.rem(lax.broadcasted_iota(jnp.int32, (block, width), 1), points)
    mask = (place < lengths[...]).astype(F32)
    mask_ref[...] = mask
    rhs = mask * (dot_full(targets[...], repeat) - prior[...] - jnp.sqrt(noise_cols) * draw[...])
    rhs_ref[...] = rhs
    v0[r] = dot_full(rhs, mix_ref[...])
    spread_start(v0, v_send.at[0], v_recv.at[0])

    def keep_split(j):
        if keep:
            high, low = split(ncol[j])
            nch[j] = high
            ncl[j] = low

    def right(j):
        return (nch[j], ncl[j]) if keep else split(ncol[j])

    keep_split(r)
    spread_forward(ncol, n_send, n_recv, keep_split)
    spread_rest(ncol, n_send, n_recv, keep_split)

    def build(at):
        left = split(nrow[at])
        for j in range(rows):
            tile = cubic(dot3(left, right(j), NT))
            high, low = split(tile)
            kh[at, :, j * block : (j + 1) * block] = high
            kl[at, :, j * block : (j + 1) * block] = low

    build(c)

    def keep_values(j):
        high, low = split(v0[j])
        here = pl.ds(pl.multiple_of(j * block, block), block)
        vh[here, :] = high
        vl[here, :] = low

    keep_values(r)
    spread_forward(v0, v_send.at[0], v_recv.at[0], keep_values)

    def build_next(k):
        build(line_wait(nrow, z_send, z_recv, k))

    loop(1, cols, build_next)
    spread_rest(v0, v_send.at[0], v_recv.at[0], keep_values)

    def apply(step):
        def one(k):
            there = lax.rem(c + k, cols)
            acc[there] = dot3((kh[there], kl[there]), (vh[...], vl[...]), NN)

            @pl.when(k < cols)
            def _():
                remote(
                    acc.at[there], got.at[step, c], rs_send.at[step, k], rs_recv.at[step, c], r, there
                ).start()

        loop(1, cols + 1, one)

    def cross(step):
        left = split(nnew[...].reshape(cols * fresh, nnew.shape[2]))
        xacc[step] = jnp.zeros(xacc.shape[1:], F32)

        def one(j):
            tile = split(cubic(dot3(left, right(j), NT)))
            here = pl.ds(pl.multiple_of(j * block, block), block)
            part = dot3(tile, (vh[here, :], vl[here, :]), NN)
            xacc[step] += part.reshape(cols, fresh, width)

        loop(0, rows, one)
        line_start(lambda there: xacc.at[step, there], xgot.at[step], xs_send.at[step], xs_recv.at[step])

    def reduced(dst, own, send, recv):
        def wait(k):
            line_wait(dst, send, recv, k)

        loop(1, cols, wait)
        dst[c] = own
        return jnp.sum(dst[...], axis=0)

    def total_start(step):
        def one(k):
            there = lax.rem(r + k, rows)
            remote(
                dots_row.at[step, r], dots_row.at[step, r], dr_send.at[step, k], dr_recv.at[step, r], there, c
            ).start()

        loop(1, rows, one)

    def total_middle(step):
        def one(k):
            j = lax.rem(r + rows - k, rows)
            remote(
                dots_row.at[step, j], dots_row.at[step, j], dr_send.at[step, k], dr_recv.at[step, j], mate, c
            ).wait_recv()

        loop(1, rows, one)
        dots_col[step, c] = jnp.sum(dots_row[step], axis=0)
        line_start(lambda there: dots_col.at[step, c], dots_col.at[step], dc_send.at[step], dc_recv.at[step])

    def total_end(step):
        def one(k):
            line_wait(dots_col.at[step], dc_send.at[step], dc_recv.at[step], k)

        loop(1, cols, one)
        return dot_full(jnp.sum(dots_col[step], axis=0), same)

    def total_close(step):
        def one(k):
            remote(
                dots_row.at[step, r], dots_row.at[step, r], dr_send.at[step, k], dr_recv.at[step, r], mate, c
            ).wait_send()

        loop(1, rows, one)
        line_end(dots_col.at[step], dc_send.at[step], dc_recv.at[step])

    def column_sums(*values):
        sums = [jnp.sum(v, axis=0, keepdims=True) for v in values]
        return jnp.concatenate(sums + [jnp.zeros((8 - len(sums), width), F32)], axis=0)

    acc = nrow
    line_end(nrow, z_send, z_recv)
    apply(0)

    def wait_new(k):
        line_wait(nnew, w_send, w_recv, k)

    loop(1, cols, wait_new)
    cross(0)
    image0 = mask_ref[...] * reduced(got.at[0], acc[c], rs_send.at[0], rs_recv.at[0]) + noise_cols * rhs_ref[...]
    image_ref[...] = image0
    dots_row[0, r] = column_sums(rhs_ref[...] * rhs_ref[...], rhs_ref[...] * image0)
    total_start(0)
    v1[r] = dot_full(image0, mix_ref[...])
    spread_start(v1, v_send.at[1], v_recv.at[1])
    total_middle(0)
    sums0 = total_end(0)
    alpha0 = sums0[0:1] / sums0[1:2]

    def keep_next(j):
        high, low = split(v0[j] - alpha0 * v1[j])
        here = pl.ds(pl.multiple_of(j * block, block), block)
        vh[here, :] = high
        vl[here, :] = low

    keep_next(r)
    spread_forward(v1, v_send.at[1], v_recv.at[1], keep_next)

    def free_acc(k):
        there = lax.rem(c + k, cols)
        remote(acc.at[there], got.at[0, c], rs_send.at[0, k], rs_recv.at[0, c], r, there).wait_send()

    loop(1, cols, free_acc)
    spread_rest(v1, v_send.at[1], v_recv.at[1], keep_next)

    apply(1)
    cross(1)
    residual = rhs_ref[...] - alpha0 * image_ref[...]
    image1 = mask_ref[...] * reduced(got.at[1], acc[c], rs_send.at[1], rs_recv.at[1]) + noise_cols * residual
    dots_row[1, r] = column_sums(
        residual * residual, residual * image1, residual * image_ref[...] + rhs_ref[...] * image1
    )
    total_start(1)
    total_middle(1)
    sums1 = total_end(1)
    ratio = sums1[0:1] / sums0[0:1]
    alpha1 = sums1[0:1] / (sums1[1:2] + ratio * (sums1[2:3] + ratio * sums0[1:2]))
    out_res[...] = residual - alpha1 * (image1 + ratio * image_ref[...])
    first = reduced(xgot.at[0], xacc[0, c], xs_send.at[0], xs_recv.at[0])
    second = reduced(xgot.at[1], xacc[1, c], xs_send.at[1], xs_recv.at[1])
    out_pred[...] = prior_new[...] + (alpha0 + alpha1 * ratio) * first + alpha1 * second

    spread_end(ncol, n_send, n_recv)
    line_end(nnew, w_send, w_recv)

    def free_last(k):
        there = lax.rem(c + k, cols)
        remote(acc.at[there], got.at[1, c], rs_send.at[1, k], rs_recv.at[1, c], r, there).wait_send()

    loop(1, cols, free_last)
    for step, buf in ((0, v0), (1, v1)):
        spread_end(buf, v_send.at[step], v_recv.at[step])
        line_end(xgot.at[step], xs_send.at[step], xs_recv.at[step])
        total_close(step)


def shards(rows, cols, features, new_features, lengths, targets, prior_train, noise_draw, prior_new, time_kernel, noise_var):
    block, depth = features.shape
    fresh = new_features.shape[0]
    width = prior_train.shape[1]
    vmem = pl.BlockSpec(memory_space=pltpu.VMEM)
    dma = pltpu.SemaphoreType.DMA
    assert depth == width
    keep = 4 * rows * cols * block * block <= 2**24
    kept = (rows, block, depth) if keep else (1, 16, depth)
    flops = 2 * 3 * block * cols * block * rows * (depth + 2 * width)
    return pl.pallas_call(
        functools.partial(body, rows, cols, keep),
        out_shape=(
            jax.ShapeDtypeStruct((block, width), F32),
            jax.ShapeDtypeStruct((fresh, width), F32),
        ),
        in_specs=[vmem] * 9,
        out_specs=(vmem, vmem),
        scratch_shapes=[
            pltpu.VMEM((rows, block, depth), F32),
            pltpu.VMEM((cols, block, depth), F32),
            pltpu.VMEM((cols, fresh, depth), F32),
            pltpu.VMEM((rows, block, width), F32),
            pltpu.VMEM((rows, block, width), F32),
            pltpu.VMEM(kept, BF16),
            pltpu.VMEM(kept, BF16),
            pltpu.VMEM((cols, block, rows * block), BF16),
            pltpu.VMEM((cols, block, rows * block), BF16),
            pltpu.VMEM((rows * block, width), BF16),
            pltpu.VMEM((rows * block, width), BF16),
            pltpu.VMEM((2, cols, fresh, width), F32),
            pltpu.VMEM((2, cols, block, width), F32),
            pltpu.VMEM((2, cols, fresh, width), F32),
            pltpu.VMEM((block, width), F32),
            pltpu.VMEM((block, width), F32),
            pltpu.VMEM((block, width), F32),
            pltpu.VMEM((width, width), F32),
            pltpu.VMEM((2, rows, 8, width), F32),
            pltpu.VMEM((2, cols, 8, width), F32),
            dma((rows,)),
            dma((rows,)),
            dma((2, rows)),
            dma((2, rows)),
            dma((cols,)),
            dma((cols,)),
            dma((cols,)),
            dma((cols,)),
            dma((2, cols)),
            dma((2, cols)),
            dma((2, cols)),
            dma((2, cols)),
            dma((2, rows)),
            dma((2, rows)),
            dma((2, cols)),
            dma((2, cols)),
        ],
        compiler_params=pltpu.CompilerParams(
            collective_id=0, has_side_effects=True, vmem_limit_bytes=63 * 2**20
        ),
        cost_estimate=pl.CostEstimate(flops=flops, bytes_accessed=8 * block * width * 4, transcendentals=0),
    )(
        features,
        new_features,
        lengths.reshape(block, 1),
        targets,
        prior_train,
        noise_draw,
        prior_new,
        time_kernel,
        noise_var.reshape(1, -1),
    )


def solution(mesh):
    both = ("row", "col")
    return jax.shard_map(
        functools.partial(shards, mesh.shape["row"], mesh.shape["col"]),
        mesh=mesh,
        in_specs=(
            P(both, None),
            P(both, None),
            P(both),
            P(both, None),
            P(both, None),
            P(both, None),
            P(both, None),
            P(),
            P(),
        ),
        out_specs=(P(both, None), P(both, None)),
        check_vma=False,
    )
```

time: 351 us -> 123 us (0.35)
  waiting for transfers between devices: 187 us -> 0 us
  Pallas kernels: 0 us -> 117 us
  blocking collectives: 92.1 us -> 0 us
  matrix products: 45.1 us -> 0 us
  between operations: 14.3 us -> 0.66 us
  other arithmetic: 8.39 us -> 0 us
    pallas_call x0 -> x1, Pallas kernels: none -> 117 us  [shards(): pl.pallas_call(functools.partial(body, rows, cols, keep), out_shape=(jax....]
    all_gather x5 -> x0, waiting for transfers between devices: 113 us -> none  [the longest x2 47.5 us: operate(): spread = lax.all_gather(mixed, 'row', axis=0, tiled=True)]
    psum x2 -> x0, blocking collectives: 77.8 us -> none  [two_products(): lax.psum((per_sample(values, values), per_sample(values, image)), ('row',...]
    reduce_scatter x3 -> x0, waiting for transfers between devices: 73.4 us -> none  [the longest x2 54.5 us: operate(): lax.psum_scatter(jnp.dot(kernel_tile, spread, precision=lax.Precision.HIG...]
    dot_general x8 -> x0, matrix products: 45.1 us -> none  [the longest x2 22.4 us: operate(): jnp.dot(kernel_tile, spread, precision=lax.Precision.HIGHEST)]
    all_gather x1 -> x0, blocking collectives: 14.4 us -> none  [shards(): lax.all_gather(normed_new, 'col', axis=0, tiled=True)]
    reduce_sum x8 -> x0, other arithmetic: 3.9 us -> none  [the longest x6 2.69 us: per_sample(): jnp.sum((first * second).reshape(first.shape[0], samples, checkpoints), a...]
    unnamed x16 -> x9, local copies, waits for them, and re-layouts: 0.04 us -> 3.8 us
  transfers between devices with their start and end apart: 8 -> 0, of which waited for: 8 -> 0; matrix products, arithmetic and copies ran while one was open for 5% -> 0% of each run, Pallas kernels for 0% -> 0%
where the time goes in v1:
time: 123 us
  Pallas kernels  117 us (95%)
  local copies, waits for them, and re-layouts  4.6 us (4%)
    pallas_call x1, Pallas kernels, shards(): pl.pallas_call(functools.partial(body, rows, cols, keep), out_shape=(jax....  117 us
    unnamed x9, local copies, waits for them, and re-layouts  3.8 us

profile of v1, /device:TPU:0, one launch (start us, length us, event | category | flops | bytes accessed | tf_op | source)
XLA Modules:
  0.0 122.6 jit_solution(3308655905232703375)
XLA Ops:
  0.6 0.0 copy-start.2
  0.6 0.7 copy-done.2
  1.3 0.0 copy-start
  1.3 0.8 copy.12.lengths
  2.1 0.0 copy-done
  2.1 0.8 copy.13.targets
  2.9 117.4 %shard_map.104 = (f32[256,256]{1,0:T(8,128)}, f32[64,256]{1,0:T(8,128)}) custom-call(f32[256,256]{1,0:T(8,128)} %feat.1, f32[64,256]{1,0:T(8,128)} %feat_new.1, s32[256,1]{1,0:T(8,128)} %copy.12.lengths, f32[256,64]{1,0:T(8,128)} %copy.13.targets, f32[256,256]{1,0:T(8,128)} %prior.1, f32[256,256]{1,0:T(8,128)} %draw.1, f32[64,256]{1,0:T(8,128)} %prior_new.1, ...), custom_call_target="tpu_custom_call" | custom-call | flops 9663676416 | bytes 2097152 | tf_op jit(solution)/shard_map/pallas_call | solution.py:406
  120.3 0.0 copy-start.1
  120.3 1.7 %copy.16 = f32[256,256]{1,0:T(8,128)} copy(f32[256,256]{1,0:T(8,128)} %get-tuple-element.4) | data formatting | bytes 524288
  122.0 0.0 copy-done.1
  122.0 0.6 copy.17
Async XLA Ops:
  0.6 0.7 copy-start.2
  1.3 0.8 copy-start
  120.3 1.7 %copy-start.1 = (f32[64,256]{1,0:T(8,128)S(1)}, f32[64,256]{1,0:T(8,128)}, u32[]{:S(2)}) copy-start(f32[64,256]{1,0:T(8,128)} %get-tuple-element.5) | copy-start | bytes 196612

commit v2 on v1

--- a/solution.py
+++ b/solution.py
@@ -197,7 +197,6 @@
 
     line_start(lambda there: nrow.at[c], nrow, z_send, z_recv)
     spread_start(ncol, n_send, n_recv)
-    line_start(lambda there: nnew.at[c], nnew, w_send, w_recv)
 
     lane = lax.broadcasted_iota(jnp.int32, (points, width), 1)
     line = lax.broadcasted_iota(jnp.int32, (points, width), 0)
@@ -253,18 +252,71 @@
     loop(1, cols, build_next)
     spread_rest(v0, v_send.at[0], v_recv.at[0], keep_values)
 
+    relay = cols == 4
+    if relay:
+        end = 1 - lax.rem((c + 1) // 2, 2)
+        near = 1 + c // 2
+        edge = 3 * (c - 1)
+        chunks = (3 - c, end * (3 - near) + (1 - end) * edge, end * near + (1 - end) * (3 - edge))
+        to = (end * near + (1 - end) * (3 - c), chunks[1], chunks[2])
+        slots = (end * near + (1 - end) * c, c, c)
+    else:
+        chunks = to = tuple(lax.rem(c + k, cols) for k in range(1, cols))
+        slots = (c,) * (cols - 1)
+
+    def chunk_copy(step, i):
+        return remote(
+            acc.at[chunks[i]], got.at[step, slots[i]], rs_send.at[step, i], rs_recv.at[step, slots[i]], r, to[i]
+        )
+
+    def arrival(step, src):
+        return remote(got.at[step, src], got.at[step, src], rs_send.at[step, 0], rs_recv.at[step, src], mate, c)
+
     def apply(step):
-        def one(k):
-            there = lax.rem(c + k, cols)
+        def product(there):
             acc[there] = dot3((kh[there], kl[there]), (vh[...], vl[...]), NN)
 
-            @pl.when(k < cols)
+        for i in range(cols - 1):
+            product(chunks[i])
+            if relay and i == 2:
+
+                @pl.when(end == 1)
+                def _():
+                    chunk_copy(step, i).start()
+
+            else:
+                chunk_copy(step, i).start()
+        product(c)
+        if relay:
+
+            @pl.when(end == 0)
             def _():
-                remote(
-                    acc.at[there], got.at[step, c], rs_send.at[step, k], rs_recv.at[step, c], r, there
-                ).start()
-
-        loop(1, cols + 1, one)
+                arrival(step, c).wait_recv()
+                acc[chunks[2]] += got[step, c]
+                chunk_copy(step, 2).start()
+
+    def gathered(step):
+        if relay:
+            arrival(step, end + (1 - end) * (3 - c)).wait_recv()
+            arrival(step, 2 * end).wait_recv()
+
+            @pl.when(end == 0)
+            def _():
+                arrival(step, 3).wait_recv()
+
+            @pl.when(end == 1)
+            def _():
+                got[step, 3 - c] = jnp.zeros(got.shape[2:], F32)
+
+        else:
+            for i in range(cols - 1):
+                arrival(step, chunks[i]).wait_recv()
+        got[step, c] = acc[c]
+        return jnp.sum(got[step], axis=0)
+
+    def chunks_end(step):
+        for i in range(cols - 1):
+            chunk_copy(step, i).wait_send()
 
     def cross(step):
         left = split(nnew[...].reshape(cols * fresh, nnew.shape[2]))
@@ -330,19 +382,20 @@
     acc = nrow
     line_end(nrow, z_send, z_recv)
     apply(0)
+    line_start(lambda there: nnew.at[c], nnew, w_send, w_recv)
 
     def wait_new(k):
         line_wait(nnew, w_send, w_recv, k)
 
-    loop(1, cols, wait_new)
-    cross(0)
-    image0 = mask_ref[...] * reduced(got.at[0], acc[c], rs_send.at[0], rs_recv.at[0]) + noise_cols * rhs_ref[...]
+    image0 = mask_ref[...] * gathered(0) + noise_cols * rhs_ref[...]
     image_ref[...] = image0
     dots_row[0, r] = column_sums(rhs_ref[...] * rhs_ref[...], rhs_ref[...] * image0)
     total_start(0)
     v1[r] = dot_full(image0, mix_ref[...])
     spread_start(v1, v_send.at[1], v_recv.at[1])
+    loop(1, cols, wait_new)
     total_middle(0)
+    cross(0)
     sums0 = total_end(0)
     alpha0 = sums0[0:1] / sums0[1:2]
 
@@ -355,17 +408,13 @@
     keep_next(r)
     spread_forward(v1, v_send.at[1], v_recv.at[1], keep_next)
 
-    def free_acc(k):
-        there = lax.rem(c + k, cols)
-        remote(acc.at[there], got.at[0, c], rs_send.at[0, k], rs_recv.at[0, c], r, there).wait_send()
-
-    loop(1, cols, free_acc)
+    chunks_end(0)
     spread_rest(v1, v_send.at[1], v_recv.at[1], keep_next)
 
     apply(1)
     cross(1)
     residual = rhs_ref[...] - alpha0 * image_ref[...]
-    image1 = mask_ref[...] * reduced(got.at[1], acc[c], rs_send.at[1], rs_recv.at[1]) + noise_cols * residual
+    image1 = mask_ref[...] * gathered(1) + noise_cols * residual
     dots_row[1, r] = column_sums(
         residual * residual, residual * image1, residual * image_ref[...] + rhs_ref[...] * image1
     )
@@ -382,11 +431,7 @@
     spread_end(ncol, n_send, n_recv)
     line_end(nnew, w_send, w_recv)
 
-    def free_last(k):
-        there = lax.rem(c + k, cols)
-        remote(acc.at[there], got.at[1, c], rs_send.at[1, k], rs_recv.at[1, c], r, there).wait_send()
-
-    loop(1, cols, free_last)
+    chunks_end(1)
     for step, buf in ((0, v0), (1, v1)):
         spread_end(buf, v_send.at[step], v_recv.at[step])
         line_end(xgot.at[step], xs_send.at[step], xs_recv.at[step])

time: 123 us -> 109 us (0.89)
  Pallas kernels: 117 us -> 104 us
    pallas_call x1, Pallas kernels: 117 us -> 104 us  [shards(): pl.pallas_call(functools.partial(body, rows, cols, keep), out_shape=(jax....]
where the time goes in v2:
time: 109 us
  Pallas kernels  104 us (95%)
  local copies, waits for them, and re-layouts  4.6 us (4%)
    pallas_call x1, Pallas kernels, shards(): pl.pallas_call(functools.partial(body, rows, cols, keep), out_shape=(jax....  104 us
    unnamed x9, local copies, waits for them, and re-layouts  3.8 us

profile of v2, /device:TPU:0, one launch (start us, length us, event | category | flops | bytes accessed | tf_op | source)
XLA Modules:
  0.0 108.8 jit_solution(14188332669777009376)
XLA Ops:
  0.6 0.0 copy-start.2
  0.6 0.7 copy-done.2
  1.3 0.0 copy-start
  1.3 0.8 copy.12.lengths
  2.1 0.0 copy-done
  2.1 0.8 copy.13.targets
  2.9 103.5 %shard_map.104 = (f32[256,256]{1,0:T(8,128)}, f32[64,256]{1,0:T(8,128)}) custom-call(f32[256,256]{1,0:T(8,128)} %feat.1, f32[64,256]{1,0:T(8,128)} %feat_new.1, s32[256,1]{1,0:T(8,128)} %copy.12.lengths, f32[256,64]{1,0:T(8,128)} %copy.13.targets, f32[256,256]{1,0:T(8,128)} %prior.1, f32[256,256]{1,0:T(8,128)} %draw.1, f32[64,256]{1,0:T(8,128)} %prior_new.1, ...), custom_call_target="tpu_custom_call" | custom-call | flops 9663676416 | bytes 2097152 | tf_op jit(solution)/shard_map/pallas_call | solution.py:451
  106.4 0.0 copy-start.1
  106.4 1.7 %copy.16 = f32[256,256]{1,0:T(8,128)} copy(f32[256,256]{1,0:T(8,128)} %get-tuple-element.4) | data formatting | bytes 524288
  108.1 0.0 copy-done.1
  108.1 0.6 copy.17
Async XLA Ops:
  0.6 0.7 copy-start.2
  1.3 0.8 copy-start
  106.4 1.7 %copy-start.1 = (f32[64,256]{1,0:T(8,128)S(1)}, f32[64,256]{1,0:T(8,128)}, u32[]{:S(2)}) copy-start(f32[64,256]{1,0:T(8,128)} %get-tuple-element.5) | copy-start | bytes 196612
